TPU v7x, 32 devices: a whole 2x2x4 slice. The times are simulated.
32 devices in a mesh: dp: 16 (over z, x, core), tensor: 2 (over y).
Axes of the slice: x: 2, y: 2, z: 4, core: 2. Of those that a mesh axis runs over, the one named last changes fastest.
Arguments:
- inputs: bfloat16 [40960, 1024], P(('dp', 'tensor')), may hold values from -6 to 6
- teacher: bfloat16 [40960, 1024], P(('dp', 'tensor')), may hold values from -6 to 6
- lengths: int32 [128], replicated, may hold values from 200 to 320, as said below
- first_gain: float32 [1024], replicated, may hold values from 0.5 to 1.5
- first_shift: float32 [1024], replicated, may hold values from -0.2 to 0.2
- query_key_value_weight: bfloat16 [3, 1024, 1024], P(None, 'dp', 'tensor'), may hold values from -0.1875 to 0.1875
- heads_bias: float32 [2, 1024], P(None, 'tensor'), may hold values from -0.2 to 0.2
- merge_weight: bfloat16 [1024, 1024], P('dp', 'tensor'), may hold values from -1.5 to 1.5
- merge_bias: float32 [1024], replicated, may hold values from -0.6 to 0.6
- second_gain: float32 [1024], replicated, may hold values from 0.5 to 1.5
- second_shift: float32 [1024], replicated, may hold values from -0.6 to 0.6
- expand_weight: bfloat16 [1024, 4096], P('dp', 'tensor'), may hold values from -0.1875 to 0.1875
- expand_bias: float32 [4096], P('tensor'), may hold values from -0.6 to 0.6
- reduce_weight: bfloat16 [1024, 4096], P('dp', 'tensor'), may hold values from -0.09375 to 0.09375
- reduce_bias: float32 [1024], replicated, may hold values from -0.6 to 0.6
Outputs:
- loss_value: float32 [], replicated
- outputs: bfloat16 [40960, 1024], P(('dp', 'tensor'))
- inputs_grad: float32 [40960, 1024], P(('dp', 'tensor'))
- first_gain_grad: float32 [1024], replicated
- first_shift_grad: float32 [1024], replicated
- heads_weight_grad: float32 [3, 1024, 1024], P(None, 'dp', 'tensor')
- heads_bias_grad: float32 [2, 1024], P(None, 'tensor')
- merge_weight_grad: float32 [1024, 1024], P('dp', 'tensor')
- merge_bias_grad: float32 [1024], replicated
- second_gain_grad: float32 [1024], replicated
- second_shift_grad: float32 [1024], replicated
- expand_weight_grad: float32 [1024, 4096], P('dp', 'tensor')
- expand_bias_grad: float32 [4096], P('tensor')
- reduce_weight_grad: float32 [1024, 4096], P('dp', 'tensor')
- reduce_bias_grad: float32 [1024], replicated
Inputs may be any that keep to these rules, and one draw needn't show every extreme that they name: `lengths`: in every draw some image has all 320 slots valid.
All inputs are finite; a program needn't handle non-finite values.
Results may differ from a plain program's by a relative error of at most 0.0095.
Values may be sent and summed in bfloat16 or wider, within the bound.
A program may use at most 320 MiB of HBM per device.

v0:
```python
from functools import partial
import math
import jax
import jax.numpy as jnp
from jax import lax
from jax.sharding import PartitionSpec as P

HD = 64
SLOTS = 320
EPSILON = 1e-05
MASKED_SCORE = -1e30


def layer_norm(rows, gain, shift):
    centre = jnp.mean(rows, axis=-1, keepdims=True)
    centred = rows - centre
    spread = jnp.mean(centred * centred, axis=-1, keepdims=True)
    return centred * lax.rsqrt(spread + EPSILON) * gain + shift


def gather_rows(values):
    return lax.all_gather(values, "tensor", axis=0, tiled=True)


def reduce_rows(values):
    return lax.psum_scatter(values, "tensor", scatter_dimension=0, tiled=True)


def fetch_mixing(query_key_value_weight, merge_weight):
    return (
        lax.all_gather(query_key_value_weight, "dp", axis=1, tiled=True),
        lax.all_gather(merge_weight, "dp", axis=0, tiled=True),
    )


def fetch_feed(expand_weight, reduce_weight):
    return (
        lax.all_gather(expand_weight, "dp", axis=0, tiled=True),
        lax.all_gather(reduce_weight, "dp", axis=0, tiled=True),
    )


def masked_scores(query_heads, key_heads, key_valid, scale):
    raw_scores = (
        jnp.einsum("bqhe,bkhe->bhqk", query_heads, key_heads, preferred_element_type=jnp.float32)
        * scale
    )
    return jnp.where(key_valid[:, None, None, :], raw_scores, MASKED_SCORE)


def body(
    inputs,
    teacher,
    lengths,
    first_gain,
    first_shift,
    query_key_value_weight,
    heads_bias,
    merge_weight,
    merge_bias,
    second_gain,
    second_shift,
    expand_weight,
    expand_bias,
    reduce_weight,
    reduce_bias,
):
    local_rows = inputs.shape[0]
    group_rows = local_rows * lax.axis_size("tensor")
    images = group_rows // SLOTS
    local_width = query_key_value_weight.shape[2]
    local_heads = local_width // HD
    scale = 1.0 / math.sqrt(HD)
    mine = lax.dynamic_slice_in_dim(lengths, lax.axis_index("dp") * images, images)
    key_valid = jnp.arange(SLOTS, dtype=jnp.int32)[None, :] < mine[:, None]
    row_valid = lax.dynamic_slice_in_dim(
        key_valid.reshape(group_rows), lax.axis_index("tensor") * local_rows, local_rows
    )
    row_valid = row_valid.astype(jnp.float32)[:, None]
    count = jnp.sum(lengths).astype(jnp.float32)
    inputs_f = inputs.astype(jnp.float32)
    normalized_rows, first_back = jax.vjp(layer_norm, inputs_f, first_gain, first_shift)
    normed_b = normalized_rows.astype(jnp.bfloat16)
    normalized_complete = gather_rows(normed_b)
    heads_complete_rows, merge_full = fetch_mixing(query_key_value_weight, merge_weight)
    projected_heads = jnp.einsum(
        "xz,ezi->exi", normalized_complete, heads_complete_rows, preferred_element_type=jnp.float32
    )
    queries = (projected_heads[0] + heads_bias[0]).astype(jnp.bfloat16)
    key_rows = projected_heads[1].astype(jnp.bfloat16)
    value_rows = (projected_heads[2] + heads_bias[1]).astype(jnp.bfloat16)
    query_heads = queries.reshape(images, SLOTS, local_heads, HD)
    key_heads = key_rows.reshape(images, SLOTS, local_heads, HD)
    value_heads = value_rows.reshape(images, SLOTS, local_heads, HD)
    scores = masked_scores(query_heads, key_heads, key_valid, scale)
    highest = jnp.max(scores, axis=-1, keepdims=True)
    expo = jnp.exp(scores - highest)
    totals = jnp.sum(expo, axis=-1, keepdims=True)
    attend = expo / totals
    log_total = highest + jnp.log(totals)
    mixed = jnp.einsum(
        "bhqk,bkhe->bqhe",
        attend.astype(jnp.bfloat16),
        value_heads,
        preferred_element_type=jnp.float32,
    )
    mixed_b = mixed.reshape(group_rows, local_width).astype(jnp.bfloat16)
    branch_part = jnp.einsum("rf,df->rd", mixed_b, merge_full, preferred_element_type=jnp.float32)
    hidden_state = inputs_f + reduce_rows(branch_part) + merge_bias
    second, second_back = jax.vjp(layer_norm, hidden_state, second_gain, second_shift)
    second_b = second.astype(jnp.bfloat16)
    second_full = gather_rows(second_b)
    expand_full, reduce_full = fetch_feed(expand_weight, reduce_weight)
    pre_act = jnp.dot(second_full, expand_full, preferred_element_type=jnp.float32) + expand_bias
    activ, gelu_back = jax.vjp(partial(jax.nn.gelu, approximate=True), pre_act)
    activ_b = activ.astype(jnp.bfloat16)
    feed_part = jnp.einsum("rf,df->rd", activ_b, reduce_full, preferred_element_type=jnp.float32)
    feed_sum = reduce_rows(feed_part)
    result = (hidden_state + feed_sum + reduce_bias) * row_valid
    error = (result - teacher.astype(jnp.float32)) * row_valid
    loss_part = jnp.sum(error * error)
    result_grad = 2.0 * error / count
    expand_back, reduce_back = fetch_feed(expand_weight, reduce_weight)
    second_src = gather_rows(second_b)
    result_full = gather_rows(result_grad.astype(jnp.bfloat16))
    activ_grad = jnp.dot(result_full, reduce_back, preferred_element_type=jnp.float32)
    reduce_grad = jnp.einsum("rd,rf->df", result_full, activ_b, preferred_element_type=jnp.float32)
    pre_grad = gelu_back(activ_grad)[0].astype(jnp.bfloat16)
    expand_bias_grad = jnp.sum(pre_grad, axis=0, dtype=jnp.float32)
    expand_grad = jnp.einsum("rd,rf->df", second_src, pre_grad, preferred_element_type=jnp.float32)
    second_grad = reduce_rows(
        jnp.einsum("rf,df->rd", pre_grad, expand_back, preferred_element_type=jnp.float32)
    )
    hidden_ln_grad, second_gain_grad, second_shift_grad = second_back(second_grad)
    hidden_grad = result_grad + hidden_ln_grad
    reduce_bias_grad = jnp.sum(result_grad, axis=0)
    merge_bias_grad = jnp.sum(hidden_grad, axis=0)
    heads_pullback_rows, merge_back = fetch_mixing(query_key_value_weight, merge_weight)
    normalized_input_rows = gather_rows(normed_b)
    hidden_full = gather_rows(hidden_grad.astype(jnp.bfloat16))
    mixed_grad = jnp.einsum(
        "rd,df->rf", hidden_full, merge_back, preferred_element_type=jnp.float32
    ).astype(jnp.bfloat16)
    merge_grad = jnp.einsum("rd,rf->df", hidden_full, mixed_b, preferred_element_type=jnp.float32)
    mixed_heads = mixed_grad.reshape(images, SLOTS, local_heads, HD)
    attend_again = jnp.exp(masked_scores(query_heads, key_heads, key_valid, scale) - log_total)
    value_grad = jnp.einsum(
        "bhqk,bqhe->bkhe",
        attend_again.astype(jnp.bfloat16),
        mixed_heads,
        preferred_element_type=jnp.float32,
    ).astype(jnp.bfloat16)
    attend_grad = jnp.einsum(
        "bqhe,bkhe->bhqk", mixed_heads, value_heads, preferred_element_type=jnp.float32
    )
    score_grad = attend_again * (
        attend_grad - jnp.sum(attend_again * attend_grad, axis=-1, keepdims=True)
    )
    score_grad = score_grad.astype(jnp.bfloat16)
    query_grad = (
        jnp.einsum("bhqk,bkhe->bqhe", score_grad, key_heads, preferred_element_type=jnp.float32)
        * scale
    ).astype(jnp.bfloat16)
    key_grad = (
        jnp.einsum("bhqk,bqhe->bkhe", score_grad, query_heads, preferred_element_type=jnp.float32)
        * scale
    ).astype(jnp.bfloat16)
    projected_heads_gradient = jnp.stack(
        [
            query_grad.reshape(group_rows, local_width),
            key_grad.reshape(group_rows, local_width),
            value_grad.reshape(group_rows, local_width),
        ]
    )
    heads_bias_grad = jnp.stack(
        [
            jnp.sum(projected_heads_gradient[0], axis=0, dtype=jnp.float32),
            jnp.sum(projected_heads_gradient[2], axis=0, dtype=jnp.float32),
        ]
    )
    heads_grad = jnp.einsum(
        "jb,mjx->mbx",
        normalized_input_rows,
        projected_heads_gradient,
        preferred_element_type=jnp.float32,
    )
    normed_grad = reduce_rows(
        jnp.einsum(
            "mex,mwx->ew",
            projected_heads_gradient,
            heads_pullback_rows,
            preferred_element_type=jnp.float32,
        )
    )
    inputs_ln_grad, first_gain_grad, first_shift_grad = first_back(normed_grad)
    inputs_grad = hidden_grad + inputs_ln_grad
    heads_grad, merge_grad = (
        lax.psum_scatter(
            heads_grad.astype(jnp.bfloat16), "dp", scatter_dimension=1, tiled=True
        ).astype(jnp.float32),
        lax.psum_scatter(
            merge_grad.astype(jnp.bfloat16), "dp", scatter_dimension=0, tiled=True
        ).astype(jnp.float32),
    )
    expand_grad, reduce_grad = (
        lax.psum_scatter(
            expand_grad.astype(jnp.bfloat16), "dp", scatter_dimension=0, tiled=True
        ).astype(jnp.float32),
        lax.psum_scatter(
            reduce_grad.astype(jnp.bfloat16), "dp", scatter_dimension=0, tiled=True
        ).astype(jnp.float32),
    )
    heads_bias_grad, expand_bias_grad = lax.psum((heads_bias_grad, expand_bias_grad), "dp")
    summed = lax.psum(
        (
            first_gain_grad,
            first_shift_grad,
            second_gain_grad,
            second_shift_grad,
            merge_bias_grad,
            reduce_bias_grad,
            loss_part,
        ),
        ("dp", "tensor"),
    )
    loss_value = summed[6] / count
    return (
        loss_value,
        result.astype(jnp.bfloat16),
        inputs_grad,
        summed[0],
        summed[1],
        heads_grad,
        heads_bias_grad,
        merge_grad,
        summed[4],
        summed[2],
        summed[3],
        expand_grad,
        expand_bias_grad,
        reduce_grad,
        summed[5],
    )


def solution(mesh):
    return jax.shard_map(
        body,
        mesh=mesh,
        in_specs=(
            P(("dp", "tensor"), None),
            P(("dp", "tensor"), None),
            P(),
            P(),
            P(),
            P(None, "dp", "tensor"),
            P(None, "tensor"),
            P("dp", "tensor"),
            P(),
            P(),
            P(),
            P("dp", "tensor"),
            P("tensor"),
            P("dp", "tensor"),
            P(),
        ),
        out_specs=(
            P(),
            P(("dp", "tensor"), None),
            P(("dp", "tensor"), None),
            P(),
            P(),
            P(None, "dp", "tensor"),
            P(None, "tensor"),
            P("dp", "tensor"),
            P(),
            P(),
            P(),
            P("dp", "tensor"),
            P("tensor"),
            P("dp", "tensor"),
            P(),
        ),
        check_vma=False,
    )
```

profile of v0, /device:TPU:0, one launch (start us, length us, event | category | flops | bytes accessed | tf_op | source)
XLA Modules:
  0.0 1575.8 jit_solution(5867062736825207133)
XLA Ops:
  17.6 69.5 %all-gather.9.cloned.1.call-done = bf16[2560,1024]{1,0:T(8,128)(2,1)} async-done(((bf16[1280,1024]{1,0:T(8,128)(2,1)}), bf16[2560,1024]{1,0:T(8,128)(2,1)}) %all-gather.9.cloned.1.call-update) | async-done | bytes 5242896 | tf_op jit(solution)/shard_map/all_gather | solution.py:22
  87.2 47.4 %all-gather.11.cloned.1.call-done = bf16[3,1024,512]{2,1,0:T(8,128)(2,1)} async-done(((bf16[3,64,512]{2,1,0:T(8,128)(2,1)}), bf16[3,1024,512]{2,1,0:T(8,128)(2,1)}) %all-gather.11.cloned.1.call-update) | async-done | bytes 3145744 | tf_op jit(solution)/shard_map/all_gather | solution.py:31
  134.6 11.3 convolution_bitcast_fusion
  153.2 9.3 fusion.60
  168.4 7.4 squeeze.7
  175.8 7.4 reshape.163
  183.2 6.9 copy.71
  196.0 7.3 squeeze.8
  212.2 16.7 %fusion.13 = (f32[8,8,320]{2,1,0:T(8,128)S(1)}, f32[8,8,320,320]{2,3,1,0:T(8,128)}) fusion(pred[8,320]{1,0:T(8,128)(4,1)S(1)} %iota_compare_fusion, bf16[8,320,8,64]{1,3,2,0:T(8,128)(2,1)S(1)} %copy-done.6, bf16[8,320,8,64]{1,0,3,2:T(8,128)(2,1)} %add_convert_fusion), kind=kOutput, calls=%fused_computation.22 | convolution fusion | flops 858501120 | bytes 31541760 | tf_op jit(solution)/shard_map/bqhe,bkhe->bhqk/dot_general | solution.py:45
  228.9 14.1 fusion
  243.0 16.4 %convert_bitcast_fusion.2 = bf16[8,320,8,64]{1,3,2,0:T(8,128)(2,1)} fusion(f32[8,8,320]{2,1,0:T(8,128)S(1)} %fusion, f32[8,8,320]{2,1,0:T(8,128)S(1)} %get-tuple-element.91, f32[8,8,320,320]{2,3,1,0:T(8,128)} %get-tuple-element.92, pred[8,320]{1,0:T(8,128)(4,1)S(1)} %iota_compare_fusion, bf16[8,320,8,64]{1,0,3,2:T(8,128)(2,1)} %add_convert_fusion.1), kind=kOutput, calls=%fused_computation.69 | convolution fusion | flops 872939520 | bytes 31623680 | tf_op jit(solution)/shard_map/bhqk,bkhe->bqhe/dot_general | solution.py:101
  270.9 8.8 fusion.61
  280.4 120.2 %reduce-scatter.8.cloned.1.call-done = f32[1280,1024]{1,0:T(8,128)} async-done(((f32[2560,1024]{1,0:T(8,128)}), f32[1280,1024]{1,0:T(8,128)}) %reduce-scatter.8.cloned.1.call-update) | async-done | bytes 5242896 | tf_op jit(solution)/shard_map/reduce_scatter | solution.py:26
  409.3 43.9 %all-gather.17.cloned.1.call-done = bf16[1024,2048]{1,0:T(8,128)(2,1)} async-done(((bf16[64,2048]{1,0:T(8,128)(2,1)}), bf16[1024,2048]{1,0:T(8,128)(2,1)}) %all-gather.17.cloned.1.call-update) | async-done | bytes 4194320 | tf_op jit(solution)/shard_map/all_gather | solution.py:38
  453.2 69.1 %all-gather.15.cloned.1.call-done = bf16[2560,1024]{1,0:T(8,128)(2,1)} async-done(((bf16[1280,1024]{1,0:T(8,128)(2,1)}), bf16[2560,1024]{1,0:T(8,128)(2,1)}) %all-gather.15.cloned.1.call-update) | async-done | bytes 5242896 | tf_op jit(solution)/shard_map/all_gather | solution.py:22
  522.3 23.8 %multiply_convert_fusion.1 = (bf16[2560,2048]{1,0:T(8,128)(2,1)}, f32[2560,2048]{1,0:T(8,128)}) fusion(f32[2048]{0:T(1024)S(1)} %copy-done.43, bf16[2560,1024]{1,0:T(8,128)(2,1)} %all-gather.15.cloned.1.call-done, bf16[1024,2048]{1,0:T(8,128)(2,1)} %all-gather.17.cloned.1.call-done), kind=kOutput, calls=%fused_computation.18 | convolution fusion | flops 10789847040 | bytes 40902656 | tf_op jit(solution)/shard_map/dot_general | solution.py:114
  546.1 29.1 %all-gather.19.cloned.1.call-done = bf16[1024,2048]{1,0:T(8,128)(2,1)} async-done(((bf16[64,2048]{1,0:T(8,128)(2,1)}), bf16[1024,2048]{1,0:T(8,128)(2,1)}) %all-gather.19.cloned.1.call-update) | async-done | bytes 4194320 | tf_op jit(solution)/shard_map/all_gather | solution.py:39
  575.2 16.7 %fusion.62 = f32[2560,1024]{1,0:T(8,128)} fusion(bf16[2560,2048]{1,0:T(8,128)(2,1)} %get-tuple-element.93, bf16[1024,2048]{1,0:T(8,128)(2,1)} %all-gather.19.cloned.1.call-done), kind=kOutput, calls=%fused_computation.111 | convolution fusion | flops 10737418240 | bytes 25165824 | tf_op jit(solution)/shard_map/rf,df->rd/dot_general | solution.py:117
  594.0 118.4 %reduce-scatter.10.cloned.1.call-done = f32[1280,1024]{1,0:T(8,128)} async-done(((f32[2560,1024]{1,0:T(8,128)}), f32[1280,1024]{1,0:T(8,128)}) %reduce-scatter.10.cloned.1.call-update) | async-done | bytes 5242896 | tf_op jit(solution)/shard_map/reduce_scatter | solution.py:26
  712.4 6.3 fusion.54
  726.7 68.7 %all-gather.21.cloned.1.call-done = bf16[2560,1024]{1,0:T(8,128)(2,1)} async-done(((bf16[1280,1024]{1,0:T(8,128)(2,1)}), bf16[2560,1024]{1,0:T(8,128)(2,1)}) %all-gather.21.cloned.1.call-update) | async-done | bytes 5242896 | tf_op jit(solution)/shard_map/all_gather | solution.py:22
  795.3 29.0 %convert_reduce_fusion = (f32[2048]{0:T(1024)}, bf16[2560,2048]{1,0:T(8,128)(2,1)S(1)}) fusion(f32[2560,2048]{1,0:T(8,128)} %get-tuple-element.94, f32[2048]{0:T(1024)S(1)} %copy-done.43, bf16[2560,1024]{1,0:T(8,128)(2,1)} %all-gather.21.cloned.1.call-done, bf16[1024,2048]{1,0:T(8,128)(2,1)} %all-gather.19.cloned.1.call-done), kind=kOutput, calls=%fused_computation.17 | convolution fusion | flops 10858002432 | bytes 40910848 | tf_op jit(solution)/shard_map/dot_general | solution.py:126
  828.2 14.5 fusion.63
  842.8 122.0 %reduce-scatter.12.cloned.1.call-done = f32[1280,1024]{1,0:T(8,128)} async-done(((f32[2560,1024]{1,0:T(8,128)}), f32[1280,1024]{1,0:T(8,128)}) %reduce-scatter.12.cloned.1.call-update) | async-done | bytes 5242896 | tf_op jit(solution)/shard_map/reduce_scatter | solution.py:26
  980.0 17.0 %convolution_convert_fusion.1 = bf16[1024,2048]{1,0:T(8,128)(2,1)} fusion(bf16[2560,1024]{1,0:T(8,128)(2,1)} %all-gather.21.cloned.1.call-done, bf16[2560,2048]{1,0:T(8,128)(2,1)} %get-tuple-element.93), kind=kOutput, calls=%fused_computation.63 | convolution fusion | flops 10739515392 | bytes 19922944 | tf_op jit(solution)/shard_map/rd,rf->df/dot_general | solution.py:127
  997.2 16.8 %convolution_convert_fusion.2 = bf16[1024,2048]{1,0:T(8,128)(2,1)} fusion(bf16[2560,1024]{1,0:T(8,128)(2,1)} %all-gather.15.cloned.1.call-done, bf16[2560,2048]{1,0:T(8,128)(2,1)} %copy-done.47), kind=kOutput, calls=%fused_computation.64 | convolution fusion | flops 10739515392 | bytes 19922944 | tf_op jit(solution)/shard_map/rd,rf->df/dot_general | solution.py:130
  1014.3 34.4 %all-gather.23.cloned.1.call-done = bf16[2560,1024]{1,0:T(8,128)(2,1)} async-done(((bf16[1280,1024]{1,0:T(8,128)(2,1)}), bf16[2560,1024]{1,0:T(8,128)(2,1)}) %all-gather.23.cloned.1.call-update) | async-done | bytes 5242896 | tf_op jit(solution)/shard_map/all_gather | solution.py:22
  1058.9 7.2 copy.76
  1066.1 24.7 %multiply_reduce_fusion = (f32[8,8,320]{2,1,0:T(8,128)S(1)}, f32[8,8,320,320]{2,3,1,0:T(8,128)}) fusion(f32[8,8,320]{2,1,0:T(8,128)S(1)} %log_add_fusion, f32[8,8,320,320]{2,3,1,0:T(8,128)} %get-tuple-element.92, pred[8,320]{1,0:T(8,128)(4,1)S(1)} %iota_compare_fusion, bf16[8,320,8,64]{1,3,2,0:T(8,128)(2,1)} %copy.76, bf16[8,320,8,64]{1,0,3,2:T(8,128)(2,1)S(1)} %copy-done.11), kind=kOutput, calls=%fused_computation.1 | convolution fusion | flops 871608320 | bytes 57838080 | tf_op jit(solution)/shard_map/bqhe,bkhe->bhqk/dot_general | solution.py:153
  1090.9 26.7 %multiply_convert_fusion = bf16[8,8,320,320]{2,3,1,0:T(8,128)(2,1)} fusion(f32[8,8,320,320]{2,3,1,0:T(8,128)} %get-tuple-element.96, f32[8,8,320]{2,1,0:T(8,128)S(1)} %get-tuple-element.95, f32[8,8,320]{2,1,0:T(8,128)S(1)} %log_add_fusion, f32[8,8,320,320]{2,3,1,0:T(8,128)} %get-tuple-element.92, pred[8,320]{1,0:T(8,128)(4,1)S(1)} %iota_compare_fusion), kind=kLoop, calls=%fused_computation | loop fusion | flops 39321600 | bytes 65702400 | tf_op jit(solution)/shard_map/convert_element_type | solution.py:159
  1117.6 15.0 convert_reduce_fusion.2
  1132.6 6.9 copy.100
  1139.5 8.2 reshape.161
  1147.7 9.9 fusion.30
  1157.6 6.8 copy.99
  1164.4 8.0 reshape.160
  1172.4 10.3 convert_reduce_fusion.3
  1182.7 6.7 copy.98
  1189.5 8.0 reshape.159
  1203.4 8.8 convert_bitcast_fusion
  1218.2 7.3 convolution_convert_fusion.3
  1225.7 13.0 convolution_bitcast_fusion.1
  1244.4 61.5 %all-reduce.2 = (f32[2,512]{1,0:T(2,128)}, f32[2048]{0:T(1024)}) all-reduce(f32[2,512]{1,0:T(2,128)S(1)} %pad_maximum_fusion, f32[2048]{0:T(1024)S(1)} %copy-done.35), channel_id=1, replica_groups=mesh['dp'=16,'tensor'=2] {'dp'}, use_global_device_ids=true, to_apply=%region_25.26 | all-reduce | flops 3072 | bytes 24576 | tf_op jit(solution)/shard_map/psum | solution.py:213
  1305.9 24.2 %all-reduce.5.cloned.1.call-done = bf16[3,1024,512]{2,0,1:T(4,128)(2,1)} async-done(((bf16[3,1024,512]{2,0,1:T(4,128)(2,1)}), bf16[3,1024,512]{2,0,1:T(4,128)(2,1)}) %all-reduce.5.cloned.1.call-update) | async-done | bytes 3145744
  1332.0 58.4 %reduce-scatter.16.cloned.1.call-done = bf16[64,512]{1,0:T(8,128)(2,1)} async-done(((bf16[1024,512]{1,0:T(8,128)(2,1)}), bf16[64,512]{1,0:T(8,128)(2,1)}) %reduce-scatter.16.cloned.1.call-update) | async-done | bytes 65552 | tf_op jit(solution)/shard_map/reduce_scatter | solution.py:201
  1391.9 121.6 %reduce-scatter.14.cloned.1.call-done = f32[1280,1024]{1,0:T(8,128)} async-done(((f32[2560,1024]{1,0:T(8,128)}), f32[1280,1024]{1,0:T(8,128)}) %reduce-scatter.14.cloned.1.call-update) | async-done | bytes 5242896 | tf_op jit(solution)/shard_map/reduce_scatter | solution.py:26
  1520.6 40.2 %all-reduce.1 = (f32[]{:T(128)}, f32[1024]{0:T(1024)}, f32[1024]{0:T(1024)}, f32[1024]{0:T(1024)}, f32[1024]{0:T(1024)}, /*index=5*/f32[1024]{0:T(1024)}, f32[1024]{0:T(1024)}) all-reduce(f32[]{:T(128)} %get-tuple-element.90, f32[1024]{0:T(1024)S(1)} %get-tuple-element.62, ...), channel_id=1, replica_groups=mesh['dp'=16,'tensor'=2] {'dp','tensor'}, use_global_device_ids=true, to_apply=%region_9.10 | all-reduce | flops 6145 | bytes 49160 | tf_op jit(solution)/shard_map/psum | solution.py:214
  1561.4 6.5 add_add_fusion.2
  (194 shorter events, 125.2 us)
Async XLA Ops:
  7.2 6.2 copy-start.1
  7.2 6.2 copy-start.28
  7.2 6.2 copy-start.36
  7.2 80.0 %all-gather.9.cloned.1.call-start = ((), (), s32[]{:S(2)}) async-start(), calls=%async_computation.7 | async-start | bytes 7864320 | tf_op jit(solution)/shard_map/all_gather | solution.py:22
  9.6 7.7 copy-start.44
  9.6 7.9 copy-start.40
  15.8 118.8 %all-gather.11.cloned.1.call-start = ((), (), s32[]{:S(2)}) async-start(), calls=%async_computation.8 | async-start | bytes 3342336 | tf_op jit(solution)/shard_map/all_gather | solution.py:31
  16.5 254.4 %all-gather.13.cloned.1.call-start = ((), (), s32[]{:S(2)}) async-start(), calls=%async_computation.9 | async-start | bytes 1114112 | tf_op jit(solution)/shard_map/all_gather | solution.py:32
  17.2 383.4 %reduce-scatter.8.cloned.1.call-start = ((), (), s32[]{:S(2)}) async-start(), calls=%async_computation.10 | async-start | bytes 15728640 | tf_op jit(solution)/shard_map/reduce_scatter | solution.py:26
  145.9 5.5 copy-start.13
  203.4 5.8 copy-start.9
  228.9 14.1 copy-start.17
  243.0 16.5 %copy-start.20 = (f32[8,8,320]{2,1,0:T(8,128)}, f32[8,8,320]{2,1,0:T(8,128)S(1)}, u32[]{:S(2)}) copy-start(f32[8,8,320]{2,1,0:T(8,128)S(1)} %fusion) | copy-start | bytes 245764
  279.7 120.9 %copy-start.37 = (f32[1024]{0:T(1024)S(1)}, f32[1024]{0:T(1024)}, u32[]{:S(2)}) copy-start(f32[1024]{0:T(1024)} %param.23) | copy-start | bytes 12292
  279.8 173.5 %all-gather.17.cloned.1.call-start = ((), (), s32[]{:S(2)}) async-start(), calls=%async_computation.12 | async-start | bytes 4456448 | tf_op jit(solution)/shard_map/all_gather | solution.py:38
  280.4 241.9 %all-gather.15.cloned.1.call-start = ((), (), s32[]{:S(2)}) async-start(), calls=%async_computation.11 | async-start | bytes 7864320 | tf_op jit(solution)/shard_map/all_gather | solution.py:22
  406.2 116.1 %copy-start.43 = (f32[2048]{0:T(1024)S(1)}, f32[2048]{0:T(1024)}, u32[]{:S(2)}) copy-start(f32[2048]{0:T(1024)} %param.27) | copy-start | bytes 24580
  408.5 166.7 %all-gather.19.cloned.1.call-start = ((), (), s32[]{:S(2)}) async-start(), calls=%async_computation.13 | async-start | bytes 4456448 | tf_op jit(solution)/shard_map/all_gather | solution.py:39
  409.2 303.2 %reduce-scatter.10.cloned.1.call-start = ((), (), s32[]{:S(2)}) async-start(), calls=%async_computation.14 | async-start | bytes 15728640 | tf_op jit(solution)/shard_map/reduce_scatter | solution.py:26
  591.9 120.6 %copy-start.39 = (f32[1024]{0:T(1024)S(1)}, f32[1024]{0:T(1024)}, u32[]{:S(2)}) copy-start(f32[1024]{0:T(1024)} %param.29) | copy-start | bytes 12292
  591.9 203.4 %all-gather.21.cloned.1.call-start = ((), (), s32[]{:S(2)}) async-start(), calls=%async_computation.15 | async-start | bytes 7864320 | tf_op jit(solution)/shard_map/all_gather | solution.py:22
  594.0 124.8 %copy-start.16 = (bf16[1280,1024]{1,0:T(8,128)(2,1)S(1)}, bf16[1280,1024]{1,0:T(8,128)(2,1)}, u32[]{:S(2)}) copy-start(bf16[1280,1024]{1,0:T(8,128)(2,1)} %param.16) | copy-start | bytes 7864324
  726.6 238.1 %reduce-scatter.12.cloned.1.call-start = ((), (), s32[]{:S(2)}) async-start(), calls=%async_computation.16 | async-start | bytes 15728640 | tf_op jit(solution)/shard_map/reduce_scatter | solution.py:26
  795.3 32.8 %copy-start.41 = (bf16[1024,2048]{1,0:T(8,128)(2,1)S(1)}, bf16[1024,2048]{1,0:T(8,128)(2,1)}, u32[]{:S(2)}) copy-start(bf16[1024,2048]{1,0:T(8,128)(2,1)} %all-gather.17.cloned.1.call-done) | copy-start | bytes 12582916
  842.7 206.0 %all-gather.23.cloned.1.call-start = ((), (), s32[]{:S(2)}) async-start(), calls=%async_computation.17 | async-start | bytes 7864320 | tf_op jit(solution)/shard_map/all_gather | solution.py:22
  964.7 5.8 copy-start.10
  964.7 9.7 slice-start
  980.0 17.2 %copy-start.18 = (f32[8,8,320]{2,1,0:T(8,128)S(1)}, f32[8,8,320]{2,1,0:T(8,128)}, u32[]{:S(2)}) copy-start(f32[8,8,320]{2,1,0:T(8,128)} %copy-done.17) | copy-start | bytes 245764
  980.0 17.2 %copy-start.21 = (f32[8,8,320]{2,1,0:T(8,128)S(1)}, f32[8,8,320]{2,1,0:T(8,128)}, u32[]{:S(2)}) copy-start(f32[8,8,320]{2,1,0:T(8,128)} %copy-done.20) | copy-start | bytes 245764
  980.0 260.6 %reduce-scatter.20.cloned.1.call-start = ((), (), s32[]{:S(2)}) async-start(), calls=%async_computation.21 | async-start | bytes 4456448 | tf_op jit(solution)/shard_map/reduce_scatter | solution.py:209
  997.1 245.3 %reduce-scatter.18.cloned.1.call-start = ((), (), s32[]{:S(2)}) async-start(), calls=%async_computation.20 | async-start | bytes 4456448 | tf_op jit(solution)/shard_map/reduce_scatter | solution.py:206
  1014.1 316.1 %all-reduce.5.cloned.1.call-start = ((), (), s32[]{:S(2)}) async-start(), calls=%async_computation.22 | async-start | bytes 8388608
  1058.9 7.2 copy-start.11
  1090.9 26.7 %copy-start.12 = (bf16[8,320,8,64]{1,3,2,0:T(8,128)(2,1)S(1)}, bf16[8,320,8,64]{1,3,2,0:T(8,128)(2,1)}, u32[]{:S(2)}) copy-start(bf16[8,320,8,64]{1,3,2,0:T(8,128)(2,1)} %copy.76) | copy-start | bytes 7864324
  1139.5 8.2 copy-start.8
  1164.4 8.0 copy-start.7
  1189.5 10.1 copy-start.15
  1197.5 5.9 slice-start.2
  1218.0 7.7 copy-start.42
  1218.0 172.4 %reduce-scatter.16.cloned.1.call-start = ((), (), s32[]{:S(2)}) async-start(), calls=%async_computation.19 | async-start | bytes 1114112 | tf_op jit(solution)/shard_map/reduce_scatter | solution.py:201
  1225.6 287.9 %reduce-scatter.14.cloned.1.call-start = ((), (), s32[]{:S(2)}) async-start(), calls=%async_computation.18 | async-start | bytes 15728640 | tf_op jit(solution)/shard_map/reduce_scatter | solution.py:26
  1238.7 5.7 copy-start.35
  1238.7 274.8 %copy-start.2 = (bf16[1280,1024]{1,0:T(8,128)(2,1)S(1)}, bf16[1280,1024]{1,0:T(8,128)(2,1)}, u32[]{:S(2)}) copy-start(bf16[1280,1024]{1,0:T(8,128)(2,1)} %param.15) | copy-start | bytes 7864324
  1238.7 274.8 %copy-start.23 = (f32[1280]{0:T(1024)S(1)}, f32[1280]{0:T(1024)}, u32[]{:S(2)}) copy-start(f32[1280]{0:T(1024)} %copy-done.22) | copy-start | bytes 15364
  1238.7 274.8 %copy-start.29 = (f32[1024]{0:T(1024)S(1)}, f32[1024]{0:T(1024)}, u32[]{:S(2)}) copy-start(f32[1024]{0:T(1024)} %param.18) | copy-start | bytes 12292
  1242.4 275.0 %copy-start.27 = (f32[1280]{0:T(1024)S(1)}, f32[1280]{0:T(1024)}, u32[]{:S(2)}) copy-start(f32[1280]{0:T(1024)} %copy-done.26) | copy-start | bytes 15364
  1242.4 275.0 %copy-start.25 = (f32[1280]{0:T(1024)S(1)}, f32[1280]{0:T(1024)}, u32[]{:S(2)}) copy-start(f32[1280]{0:T(1024)} %copy-done.24) | copy-start | bytes 15364
  1513.5 4.0 copy-start.4
  (20 other events, 50.7 us)
Sparse Core Ops, SparseCore 0:
  15.9 71.2 all-gather.8
  89.4 45.1 all-gather.10
  136.8 36.7 all-gather.12
  279.9 120.7 reduce-scatter.7
  402.7 50.5 all-gather.16
  455.2 67.0 all-gather.14
  524.5 50.7 all-gather.18
  592.0 120.3 reduce-scatter.9
  726.7 68.5 all-gather.20
  842.8 121.8 reduce-scatter.11
  980.1 68.5 all-gather.22
  1052.4 72.4 reduce-scatter.19
  1129.2 71.3 reduce-scatter.17
  1218.1 111.9 all-reduce.4
  1334.0 56.3 reduce-scatter.15
  1392.5 120.8 reduce-scatter.13
where the time goes:
time: 1590 us; the launch traced here: 1580 us
  waiting for transfers between devices  930 us (58%)
  matrix products  266 us (17%)
  local copies, waits for them, and re-layouts  154 us (10%)
  other arithmetic  105 us (7%)
  blocking collectives  102 us (6%)
  between operations  17.8 us (1%)
    reduce_scatter x4, waiting for transfers between devices, reduce_rows(): return lax.psum_scatter(values, 'tensor', scatter_dimension=0, tiled=True)  482 us
    all_gather x4, waiting for transfers between devices, gather_rows(): return lax.all_gather(values, 'tensor', axis=0, tiled=True)  242 us
    psum x1, blocking collectives, body(): lax.psum((heads_bias_grad, expand_bias_grad), 'dp')  61.5 us
    reduce_scatter x1, waiting for transfers between devices, body(): lax.psum_scatter(merge_grad.astype(jnp.bfloat16), 'dp', scatter_dimension...  58.4 us
    all_gather x1, waiting for transfers between devices, fetch_mixing(): lax.all_gather(query_key_value_weight, 'dp', axis=1, tiled=True)  47.4 us
    another operation x7, local copies, waits for them, and re-layouts, body(): jnp.stack([query_grad.reshape(group_rows, local_width), key_grad.reshape(...  44.8 us
    all_gather x1, waiting for transfers between devices, fetch_feed(): lax.all_gather(expand_weight, 'dp', axis=0, tiled=True)  43.9 us
    psum x1, blocking collectives, body(): lax.psum((first_gain_grad, first_shift_grad, second_gain_grad, second_shi...  40.2 us
  transfers between devices with their start and end apart: 16, of which 13 were waited for; matrix products, arithmetic and copies ran while one was open for 25% of the time, Pallas kernels for 0%

commit v1 on v0

--- a/solution.py
+++ b/solution.py
@@ -11,6 +11,19 @@
 MASKED_SCORE = -1e30
 
 
+def ring_gather(x, axis, dim):
+    ways = lax.axis_size(axis)
+    up = [(d, (d + 1) % ways) for d in range(ways)]
+    down = [(d, (d - 1) % ways) for d in range(ways)]
+    earlier, later = ([x], [x])
+    for _ in range(ways // 2):
+        earlier.append(lax.ppermute(earlier[-1], axis, up))
+    for _ in range((ways - 1) // 2):
+        later.append(lax.ppermute(later[-1], axis, down))
+    line = jnp.concatenate([*earlier[::-1], *later[1:]], axis=dim)
+    return jnp.roll(line, (lax.axis_index(axis) - ways // 2) * x.shape[dim], axis=dim)
+
+
 def layer_norm(rows, gain, shift):
     centre = jnp.mean(rows, axis=-1, keepdims=True)
     centred = rows - centre
@@ -28,7 +41,7 @@
 
 def fetch_mixing(query_key_value_weight, merge_weight):
     return (
-        lax.all_gather(query_key_value_weight, "dp", axis=1, tiled=True),
+        ring_gather(query_key_value_weight, "dp", 1),
         lax.all_gather(merge_weight, "dp", axis=0, tiled=True),
     )
 

time: 1590 us -> 1540 us (0.969)
  waiting for transfers between devices: 930 us -> 858 us
  starting transfers between devices: 1.04 us -> 41.7 us
  local copies, waits for them, and re-layouts: 154 us -> 132 us
  matrix products: 266 us -> 282 us
    all_gather x4, waiting for transfers between devices: 242 us -> 172 us  [gather_rows(): return lax.all_gather(values, 'tensor', axis=0, tiled=True)]
    all_gather x1 -> x0, waiting for transfers between devices: 47.4 us -> none  [fetch_mixing(): lax.all_gather(query_key_value_weight, 'dp', axis=1, tiled=True)]
    ppermute x0 -> x15, starting transfers between devices: none -> 41.1 us  [the longest x8 26.9 us: ring_gather(): earlier.append(lax.ppermute(earlier[-1], axis, up))]
    ppermute x0 -> x15, waiting for transfers between devices: none -> 40.4 us  [the longest x8 40.4 us: ring_gather(): earlier.append(lax.ppermute(earlier[-1], axis, up))]
  transfers between devices with their start and end apart: 16 -> 30, of which waited for: 13 -> 19; matrix products, arithmetic and copies ran while one was open for 25% -> 25% of each run, Pallas kernels for 0% -> 0%
where the time goes in v1:
time: 1540 us; the launch traced here: 1530 us
  waiting for transfers between devices  858 us (56%)
  matrix products  282 us (18%)
  local copies, waits for them, and re-layouts  132 us (9%)
  blocking collectives  102 us (7%)
  other arithmetic  99.4 us (6%)
  starting transfers between devices  41.7 us (3%)
  between operations  18 us (1%)
    reduce_scatter x4, waiting for transfers between devices, reduce_rows(): return lax.psum_scatter(values, 'tensor', scatter_dimension=0, tiled=True)  489 us
    all_gather x4, waiting for transfers between devices, gather_rows(): return lax.all_gather(values, 'tensor', axis=0, tiled=True)  172 us
    psum x1, blocking collectives, body(): lax.psum((heads_bias_grad, expand_bias_grad), 'dp')  61.8 us
    reduce_scatter x1, waiting for transfers between devices, body(): lax.psum_scatter(merge_grad.astype(jnp.bfloat16), 'dp', scatter_dimension...  58.4 us
    all_gather x1, waiting for transfers between devices, fetch_feed(): lax.all_gather(expand_weight, 'dp', axis=0, tiled=True)  43.9 us
    another operation x7, local copies, waits for them, and re-layouts, body(): jnp.stack([query_grad.reshape(group_rows, local_width), key_grad.reshape(...  42.8 us
    ppermute x8, waiting for transfers between devices, ring_gather(): earlier.append(lax.ppermute(earlier[-1], axis, up))  40.4 us
    psum x1, blocking collectives, body(): lax.psum((first_gain_grad, first_shift_grad, second_gain_grad, second_shi...  40.2 us
  transfers between devices with their start and end apart: 30, of which 19 were waited for; matrix products, arithmetic and copies ran while one was open for 25% of the time, Pallas kernels for 0%

profile of v1, /device:TPU:0, one launch (start us, length us, event | category | flops | bytes accessed | tf_op | source)
XLA Modules:
  0.0 1532.4 jit_solution(8626893869269173160)
XLA Ops:
  76.0 5.9 collective-permute-start.6
  86.2 7.0 collective-permute-start.7
  97.0 8.2 concatenate.7
  105.2 15.5 %convolution_bitcast_fusion = f32[3,2560,512]{1,2,0:T(8,128)} fusion(bf16[2560,1024]{1,0:T(8,128)(2,1)} %all-gather.8.cloned.1.call-done, s32[]{:T(128)S(6)} %select_n.25, bf16[3,1024,512]{1,2,0:T(8,128)(2,1)} %concatenate.7), kind=kOutput, calls=%fused_computation.23 | convolution fusion | flops 8059355136 | bytes 24117252 | tf_op jit(solution)/shard_map/xz,ezi->exi/dot_general | solution.py:99
  124.9 8.8 fusion.65
  133.7 5.9 convert_element_type.127
  139.6 7.3 squeeze.7
  147.0 7.4 squeeze.8
  154.3 16.5 %fusion.13 = (f32[8,8,320]{2,1,0:T(8,128)S(1)}, f32[8,8,320,320]{2,3,1,0:T(8,128)}) fusion(pred[8,320]{1,0:T(8,128)(4,1)S(1)} %iota_compare_fusion, bf16[8,320,8,64]{1,0,3,2:T(8,128)(2,1)} %convert_element_type.127, f32[8,320,8,64]{1,0,3,2:T(8,128)} %squeeze.8, f32[8,64]{1,0:T(8,128)S(1)} %add.165), kind=kOutput, calls=%fused_computation.22 | convolution fusion | flops 861122560 | bytes 34165248 | tf_op jit(solution)/shard_map/bqhe,bkhe->bhqk/dot_general | solution.py:58
  170.8 14.1 fusion
  185.0 17.7 %convert_bitcast_fusion.2 = bf16[8,320,8,64]{1,3,2,0:T(8,128)(2,1)} fusion(f32[8,8,320]{2,1,0:T(8,128)S(1)} %fusion, f32[8,8,320]{2,1,0:T(8,128)S(1)} %get-tuple-element.92, f32[8,8,320,320]{2,3,1,0:T(8,128)} %get-tuple-element.93, pred[8,320]{1,0:T(8,128)(4,1)S(1)} %iota_compare_fusion, f32[8,320,8,64]{1,0,3,2:T(8,128)} %squeeze.7, f32[8,64]{1,0:T(8,128)S(1)} %add.161), kind=kOutput, calls=%fused_computation.74 | convolution fusion | flops 875560960 | bytes 34247168 | tf_op jit(solution)/shard_map/bhqk,bkhe->bqhe/dot_general | solution.py:114
  214.0 8.8 fusion.66
  223.4 127.3 %reduce-scatter.8.cloned.1.call-done = f32[1280,1024]{1,0:T(8,128)} async-done(((f32[2560,1024]{1,0:T(8,128)}), f32[1280,1024]{1,0:T(8,128)}) %reduce-scatter.8.cloned.1.call-update) | async-done | bytes 5242896 | tf_op jit(solution)/shard_map/reduce_scatter | solution.py:39
  359.5 43.9 %all-gather.14.cloned.1.call-done = bf16[1024,2048]{1,0:T(8,128)(2,1)} async-done(((bf16[64,2048]{1,0:T(8,128)(2,1)}), bf16[1024,2048]{1,0:T(8,128)(2,1)}) %all-gather.14.cloned.1.call-update) | async-done | bytes 4194320 | tf_op jit(solution)/shard_map/all_gather | solution.py:51
  403.4 69.1 %all-gather.12.cloned.1.call-done = bf16[2560,1024]{1,0:T(8,128)(2,1)} async-done(((bf16[1280,1024]{1,0:T(8,128)(2,1)}), bf16[2560,1024]{1,0:T(8,128)(2,1)}) %all-gather.12.cloned.1.call-update) | async-done | bytes 5242896 | tf_op jit(solution)/shard_map/all_gather | solution.py:35
  472.5 23.8 %multiply_convert_fusion.1 = (bf16[2560,2048]{1,0:T(8,128)(2,1)}, f32[2560,2048]{1,0:T(8,128)}) fusion(f32[2048]{0:T(1024)S(1)} %copy-done.50, bf16[2560,1024]{1,0:T(8,128)(2,1)} %all-gather.12.cloned.1.call-done, bf16[1024,2048]{1,0:T(8,128)(2,1)} %all-gather.14.cloned.1.call-done), kind=kOutput, calls=%fused_computation.18 | convolution fusion | flops 10789847040 | bytes 40902656 | tf_op jit(solution)/shard_map/dot_general | solution.py:127
  496.3 29.0 %all-gather.16.cloned.1.call-done = bf16[1024,2048]{1,0:T(8,128)(2,1)} async-done(((bf16[64,2048]{1,0:T(8,128)(2,1)}), bf16[1024,2048]{1,0:T(8,128)(2,1)}) %all-gather.16.cloned.1.call-update) | async-done | bytes 4194320 | tf_op jit(solution)/shard_map/all_gather | solution.py:52
  525.2 16.6 %fusion.67 = f32[2560,1024]{1,0:T(8,128)} fusion(bf16[2560,2048]{1,0:T(8,128)(2,1)} %get-tuple-element.94, bf16[1024,2048]{1,0:T(8,128)(2,1)} %all-gather.16.cloned.1.call-done), kind=kOutput, calls=%fused_computation.114 | convolution fusion | flops 10737418240 | bytes 25165824 | tf_op jit(solution)/shard_map/rf,df->rd/dot_general | solution.py:130
  543.9 118.4 %reduce-scatter.10.cloned.1.call-done = f32[1280,1024]{1,0:T(8,128)} async-done(((f32[2560,1024]{1,0:T(8,128)}), f32[1280,1024]{1,0:T(8,128)}) %reduce-scatter.10.cloned.1.call-update) | async-done | bytes 5242896 | tf_op jit(solution)/shard_map/reduce_scatter | solution.py:39
  662.3 6.3 fusion.59
  676.8 68.7 %all-gather.18.cloned.1.call-done = bf16[2560,1024]{1,0:T(8,128)(2,1)} async-done(((bf16[1280,1024]{1,0:T(8,128)(2,1)}), bf16[2560,1024]{1,0:T(8,128)(2,1)}) %all-gather.18.cloned.1.call-update) | async-done | bytes 5242896 | tf_op jit(solution)/shard_map/all_gather | solution.py:35
  745.4 28.8 %convert_reduce_fusion = (f32[2048]{0:T(1024)}, bf16[2560,2048]{1,0:T(8,128)(2,1)S(1)}) fusion(f32[2560,2048]{1,0:T(8,128)} %get-tuple-element.95, f32[2048]{0:T(1024)S(1)} %copy-done.50, bf16[2560,1024]{1,0:T(8,128)(2,1)} %all-gather.18.cloned.1.call-done, bf16[1024,2048]{1,0:T(8,128)(2,1)} %all-gather.16.cloned.1.call-done), kind=kOutput, calls=%fused_computation.17 | convolution fusion | flops 10858002432 | bytes 40910848 | tf_op jit(solution)/shard_map/dot_general | solution.py:139
  778.1 14.3 fusion.68
  792.5 122.0 %reduce-scatter.12.cloned.1.call-done = f32[1280,1024]{1,0:T(8,128)} async-done(((f32[2560,1024]{1,0:T(8,128)}), f32[1280,1024]{1,0:T(8,128)}) %reduce-scatter.12.cloned.1.call-update) | async-done | bytes 5242896 | tf_op jit(solution)/shard_map/reduce_scatter | solution.py:39
  914.5 5.8 multiply_reduce_fusion.1
  929.7 17.0 %convolution_convert_fusion.1 = bf16[1024,2048]{1,0:T(8,128)(2,1)} fusion(bf16[2560,1024]{1,0:T(8,128)(2,1)} %all-gather.18.cloned.1.call-done, bf16[2560,2048]{1,0:T(8,128)(2,1)} %get-tuple-element.94), kind=kOutput, calls=%fused_computation.67 | convolution fusion | flops 10739515392 | bytes 19922944 | tf_op jit(solution)/shard_map/rd,rf->df/dot_general | solution.py:140
  946.9 16.9 %convolution_convert_fusion.2 = bf16[1024,2048]{1,0:T(8,128)(2,1)} fusion(bf16[2560,1024]{1,0:T(8,128)(2,1)} %all-gather.12.cloned.1.call-done, bf16[2560,2048]{1,0:T(8,128)(2,1)} %copy-done.54), kind=kOutput, calls=%fused_computation.68 | convolution fusion | flops 10739515392 | bytes 19922944 | tf_op jit(solution)/shard_map/rd,rf->df/dot_general | solution.py:143
  963.8 34.5 %all-gather.20.cloned.1.call-done = bf16[2560,1024]{1,0:T(8,128)(2,1)} async-done(((bf16[1280,1024]{1,0:T(8,128)(2,1)}), bf16[2560,1024]{1,0:T(8,128)(2,1)}) %all-gather.20.cloned.1.call-update) | async-done | bytes 5242896 | tf_op jit(solution)/shard_map/all_gather | solution.py:35
  1009.0 5.9 copy.79
  1014.9 32.4 %multiply_reduce_fusion = (f32[8,8,320]{2,1,0:T(8,128)S(1)}, f32[8,8,320,320]{2,3,1,0:T(8,128)}) fusion(f32[8,8,320]{2,1,0:T(8,128)S(1)} %log_add_fusion, f32[8,8,320,320]{2,3,1,0:T(8,128)} %get-tuple-element.93, pred[8,320]{1,0:T(8,128)(4,1)S(1)} %iota_compare_fusion, bf16[8,320,8,64]{1,3,2,0:T(8,128)(2,1)S(1)} %copy.79, f32[8,320,8,64]{1,0,3,2:T(8,128)} %squeeze.7, ...), kind=kOutput, calls=%fused_computation.1 | convolution fusion | flops 874229760 | bytes 60461568 | tf_op jit(solution)/shard_map/bqhe,bkhe->bhqk/dot_general | solution.py:166
  1047.3 26.6 %multiply_convert_fusion = bf16[8,8,320,320]{2,3,1,0:T(8,128)(2,1)} fusion(f32[8,8,320,320]{2,3,1,0:T(8,128)} %get-tuple-element.97, f32[8,8,320]{2,1,0:T(8,128)S(1)} %get-tuple-element.96, f32[8,8,320]{2,1,0:T(8,128)S(1)} %log_add_fusion, f32[8,8,320,320]{2,3,1,0:T(8,128)} %get-tuple-element.93, pred[8,320]{1,0:T(8,128)(4,1)S(1)} %iota_compare_fusion), kind=kLoop, calls=%fused_computation | loop fusion | flops 39321600 | bytes 65702400 | tf_op jit(solution)/shard_map/convert_element_type | solution.py:172
  1073.9 15.0 convert_reduce_fusion.2
  1089.0 6.8 copy.103
  1095.8 8.0 reshape.161
  1103.8 10.4 fusion.32
  1119.3 8.0 reshape.160
  1127.3 10.4 convert_reduce_fusion.3
  1137.7 6.7 copy.101
  1144.5 8.0 reshape.159
  1158.3 10.8 convert_bitcast_fusion
  1174.9 7.4 convolution_convert_fusion.3
  1182.4 13.5 convolution_bitcast_fusion.1
  1201.6 61.8 %all-reduce.2 = (f32[2,512]{1,0:T(2,128)}, f32[2048]{0:T(1024)}) all-reduce(f32[2,512]{1,0:T(2,128)S(1)} %pad_maximum_fusion, f32[2048]{0:T(1024)S(1)} %copy-done.43), channel_id=1, replica_groups=mesh['dp'=16,'tensor'=2] {'dp'}, use_global_device_ids=true, to_apply=%region_25.27 | all-reduce | flops 3072 | bytes 24576 | tf_op jit(solution)/shard_map/psum | solution.py:226
  1263.4 23.2 %all-reduce.5.cloned.1.call-done = bf16[3,1024,512]{2,0,1:T(4,128)(2,1)} async-done(((bf16[3,1024,512]{2,0,1:T(4,128)(2,1)}), bf16[3,1024,512]{2,0,1:T(4,128)(2,1)}) %all-reduce.5.cloned.1.call-update) | async-done | bytes 3145744
  1288.5 58.4 %reduce-scatter.16.cloned.1.call-done = bf16[64,512]{1,0:T(8,128)(2,1)} async-done(((bf16[1024,512]{1,0:T(8,128)(2,1)}), bf16[64,512]{1,0:T(8,128)(2,1)}) %reduce-scatter.16.cloned.1.call-update) | async-done | bytes 65552 | tf_op jit(solution)/shard_map/reduce_scatter | solution.py:214
  1348.4 121.6 %reduce-scatter.14.cloned.1.call-done = f32[1280,1024]{1,0:T(8,128)} async-done(((f32[2560,1024]{1,0:T(8,128)}), f32[1280,1024]{1,0:T(8,128)}) %reduce-scatter.14.cloned.1.call-update) | async-done | bytes 5242896 | tf_op jit(solution)/shard_map/reduce_scatter | solution.py:39
  1477.1 40.2 %all-reduce.1 = (f32[]{:T(128)}, f32[1024]{0:T(1024)}, f32[1024]{0:T(1024)}, f32[1024]{0:T(1024)}, f32[1024]{0:T(1024)}, /*index=5*/f32[1024]{0:T(1024)}, f32[1024]{0:T(1024)}) all-reduce(f32[]{:T(128)} %get-tuple-element.91, f32[1024]{0:T(1024)S(1)} %get-tuple-element.63, ...), channel_id=1, replica_groups=mesh['dp'=16,'tensor'=2] {'dp','tensor'}, use_global_device_ids=true, to_apply=%region_9.11 | all-reduce | flops 6145 | bytes 49160 | tf_op jit(solution)/shard_map/psum | solution.py:227
  1517.9 6.5 add_add_fusion.2
  (227 shorter events, 167.1 us)
Async XLA Ops:
  7.2 97.9 %all-gather.8.cloned.1.call-start = ((), (), s32[]{:S(2)}) async-start(), calls=%async_computation.7 | async-start | bytes 7864320 | tf_op jit(solution)/shard_map/all_gather | solution.py:35
  9.6 72.5 %copy-start.48 = (f32[2,512]{1,0:T(2,128)S(1)}, f32[2,512]{1,0:T(2,128)}, u32[]{:S(2)}) copy-start(f32[2,512]{1,0:T(2,128)} %param.23) | copy-start | bytes 12292
  9.6 72.6 %copy-start.51 = (s32[128]{0:T(128)S(1)}, s32[128]{0:T(128)}, u32[]{:S(2)}) copy-start(s32[128]{0:T(128)} %param.19) | copy-start | bytes 1540
  14.7 199.3 %all-gather.10.cloned.1.call-start = ((), (), s32[]{:S(2)}) async-start(), calls=%async_computation.8 | async-start | bytes 1114112 | tf_op jit(solution)/shard_map/all_gather | solution.py:45
  15.0 11.0 collective-permute-start
  15.5 11.5 collective-permute-start.8
  26.0 10.0 collective-permute-start.1
  27.0 11.0 collective-permute-start.9
  36.0 10.0 collective-permute-start.2
  38.0 10.7 collective-permute-start.10
  46.0 10.0 collective-permute-start.3
  48.7 10.7 collective-permute-start.11
  56.0 10.0 collective-permute-start.4
  59.4 11.2 collective-permute-start.12
  66.0 10.0 collective-permute-start.5
  70.6 11.8 collective-permute-start.13
  76.0 10.2 collective-permute-start.6
  82.0 268.8 %reduce-scatter.8.cloned.1.call-start = ((), (), s32[]{:S(2)}) async-start(), calls=%async_computation.9 | async-start | bytes 15728640 | tf_op jit(solution)/shard_map/reduce_scatter | solution.py:39
  82.2 102.8 %copy-start.32 = (f32[8,64]{1,0:T(8,128)}, f32[8,64]{1,0:T(8,128)S(1)}, u32[]{:S(2)}) copy-start(f32[8,64]{1,0:T(8,128)S(1)} %add.161) | copy-start | bytes 6148
  82.3 72.1 %copy-start.27 = (f32[8,64]{1,0:T(8,128)}, f32[8,64]{1,0:T(8,128)S(1)}, u32[]{:S(2)}) copy-start(f32[8,64]{1,0:T(8,128)S(1)} %add.165) | copy-start | bytes 6148
  82.3 11.0 collective-permute-start.14
  86.2 10.7 collective-permute-start.7
  170.8 14.1 copy-start.12
  185.0 17.7 %copy-start.15 = (f32[8,8,320]{2,1,0:T(8,128)}, f32[8,8,320]{2,1,0:T(8,128)S(1)}, u32[]{:S(2)}) copy-start(f32[8,8,320]{2,1,0:T(8,128)S(1)} %fusion) | copy-start | bytes 245764
  222.8 128.0 %copy-start.45 = (f32[1024]{0:T(1024)S(1)}, f32[1024]{0:T(1024)}, u32[]{:S(2)}) copy-start(f32[1024]{0:T(1024)} %param.25) | copy-start | bytes 12292
  222.8 180.6 %all-gather.14.cloned.1.call-start = ((), (), s32[]{:S(2)}) async-start(), calls=%async_computation.11 | async-start | bytes 4456448 | tf_op jit(solution)/shard_map/all_gather | solution.py:51
  223.4 249.1 %all-gather.12.cloned.1.call-start = ((), (), s32[]{:S(2)}) async-start(), calls=%async_computation.10 | async-start | bytes 7864320 | tf_op jit(solution)/shard_map/all_gather | solution.py:35
  356.4 116.1 %copy-start.50 = (f32[2048]{0:T(1024)S(1)}, f32[2048]{0:T(1024)}, u32[]{:S(2)}) copy-start(f32[2048]{0:T(1024)} %param.29) | copy-start | bytes 24580
  358.8 166.4 %all-gather.16.cloned.1.call-start = ((), (), s32[]{:S(2)}) async-start(), calls=%async_computation.12 | async-start | bytes 4456448 | tf_op jit(solution)/shard_map/all_gather | solution.py:52
  359.4 302.9 %reduce-scatter.10.cloned.1.call-start = ((), (), s32[]{:S(2)}) async-start(), calls=%async_computation.13 | async-start | bytes 15728640 | tf_op jit(solution)/shard_map/reduce_scatter | solution.py:39
  541.8 120.5 %copy-start.47 = (f32[1024]{0:T(1024)S(1)}, f32[1024]{0:T(1024)}, u32[]{:S(2)}) copy-start(f32[1024]{0:T(1024)} %param.31) | copy-start | bytes 12292
  541.8 203.6 %all-gather.18.cloned.1.call-start = ((), (), s32[]{:S(2)}) async-start(), calls=%async_computation.14 | async-start | bytes 7864320 | tf_op jit(solution)/shard_map/all_gather | solution.py:35
  543.9 124.7 %copy-start.11 = (bf16[1280,1024]{1,0:T(8,128)(2,1)S(1)}, bf16[1280,1024]{1,0:T(8,128)(2,1)}, u32[]{:S(2)}) copy-start(bf16[1280,1024]{1,0:T(8,128)(2,1)} %param.18) | copy-start | bytes 7864324
  676.7 237.8 %reduce-scatter.12.cloned.1.call-start = ((), (), s32[]{:S(2)}) async-start(), calls=%async_computation.15 | async-start | bytes 15728640 | tf_op jit(solution)/shard_map/reduce_scatter | solution.py:39
  745.4 32.7 %copy-start.49 = (bf16[1024,2048]{1,0:T(8,128)(2,1)S(1)}, bf16[1024,2048]{1,0:T(8,128)(2,1)}, u32[]{:S(2)}) copy-start(bf16[1024,2048]{1,0:T(8,128)(2,1)} %all-gather.14.cloned.1.call-done) | copy-start | bytes 12582916
  792.5 205.9 %all-gather.20.cloned.1.call-start = ((), (), s32[]{:S(2)}) async-start(), calls=%async_computation.16 | async-start | bytes 7864320 | tf_op jit(solution)/shard_map/all_gather | solution.py:35
  929.7 17.2 %copy-start.13 = (f32[8,8,320]{2,1,0:T(8,128)S(1)}, f32[8,8,320]{2,1,0:T(8,128)}, u32[]{:S(2)}) copy-start(f32[8,8,320]{2,1,0:T(8,128)} %copy-done.12) | copy-start | bytes 245764
  929.7 17.2 %copy-start.16 = (f32[8,8,320]{2,1,0:T(8,128)S(1)}, f32[8,8,320]{2,1,0:T(8,128)}, u32[]{:S(2)}) copy-start(f32[8,8,320]{2,1,0:T(8,128)} %copy-done.15) | copy-start | bytes 245764
  929.7 268.1 %reduce-scatter.20.cloned.1.call-start = ((), (), s32[]{:S(2)}) async-start(), calls=%async_computation.20 | async-start | bytes 4456448 | tf_op jit(solution)/shard_map/reduce_scatter | solution.py:222
  946.8 252.8 %reduce-scatter.18.cloned.1.call-start = ((), (), s32[]{:S(2)}) async-start(), calls=%async_computation.19 | async-start | bytes 4456448 | tf_op jit(solution)/shard_map/reduce_scatter | solution.py:219
  963.8 322.8 %all-reduce.5.cloned.1.call-start = ((), (), s32[]{:S(2)}) async-start(), calls=%async_computation.21 | async-start | bytes 8388608
  1174.9 172.0 %reduce-scatter.16.cloned.1.call-start = ((), (), s32[]{:S(2)}) async-start(), calls=%async_computation.18 | async-start | bytes 1114112 | tf_op jit(solution)/shard_map/reduce_scatter | solution.py:214
  1182.3 287.7 %reduce-scatter.14.cloned.1.call-start = ((), (), s32[]{:S(2)}) async-start(), calls=%async_computation.17 | async-start | bytes 15728640 | tf_op jit(solution)/shard_map/reduce_scatter | solution.py:39
  1195.9 274.1 %copy-start.2 = (bf16[1280,1024]{1,0:T(8,128)(2,1)S(1)}, bf16[1280,1024]{1,0:T(8,128)(2,1)}, u32[]{:S(2)}) copy-start(bf16[1280,1024]{1,0:T(8,128)(2,1)} %param.17) | copy-start | bytes 7864324
  1195.9 274.1 %copy-start.26 = (f32[1280]{0:T(1024)S(1)}, f32[1280]{0:T(1024)}, u32[]{:S(2)}) copy-start(f32[1280]{0:T(1024)} %copy-done.25) | copy-start | bytes 15364
  1195.9 274.1 %copy-start.37 = (f32[1024]{0:T(1024)S(1)}, f32[1024]{0:T(1024)}, u32[]{:S(2)}) copy-start(f32[1024]{0:T(1024)} %param.20) | copy-start | bytes 12292
  1199.6 274.2 %copy-start.35 = (f32[1280]{0:T(1024)S(1)}, f32[1280]{0:T(1024)}, u32[]{:S(2)}) copy-start(f32[1280]{0:T(1024)} %copy-done.34) | copy-start | bytes 15364
  1199.6 274.3 %copy-start.31 = (f32[1280]{0:T(1024)S(1)}, f32[1280]{0:T(1024)}, u32[]{:S(2)}) copy-start(f32[1280]{0:T(1024)} %copy-done.30) | copy-start | bytes 15364
  (39 other events, 175.5 us)
Sparse Core Ops, SparseCore 0:
  14.8 71.2 all-gather.7
  88.2 37.9 all-gather.9
  222.9 127.7 reduce-scatter.7
  352.8 50.5 all-gather.13
  405.4 67.0 all-gather.11
  474.5 50.7 all-gather.15
  541.9 120.3 reduce-scatter.9
  676.8 68.5 all-gather.17
  792.6 121.8 reduce-scatter.11
  929.8 68.5 all-gather.19
  1002.2 72.3 reduce-scatter.19
  1078.8 71.7 reduce-scatter.17
  1175.0 111.5 all-reduce.4
  1290.5 56.3 reduce-scatter.15
  1349.1 120.8 reduce-scatter.13
